TPU v7x, 32 devices: a whole 2x2x4 slice. The times are simulated.
32 devices in a mesh: group: 2 (over x), tile: 16 (over z, y, core).
Axes of the slice: x: 2, y: 2, z: 4, core: 2. Of those that a mesh axis runs over, the one named last changes fastest.
Arguments:
- wave_phase: float32 [600, 256], replicated, may hold values from -3.140625 to 3.140625
- tile_at: int32 [8, 16], replicated, may hold values from 0 to 127, as said below
- aperture_block: int32 [8], P('group'), parts along dimension 0, may hold values from 0 to 1
- source_cell: int32 [8, 2], P('group'), parts along dimension 0, may hold values from 0 to 255
- freq_index: int32 [8, 2], P('group'), parts along dimension 0, may hold values from 0 to 599
- observed: float32 [32, 2, 2, 64, 256], P(('group', 'tile')), parts along dimension 0, may hold values from -6 to 6
- image: float32 [256, 4, 1024], P(('group', 'tile')), parts along dimension 0, may hold values from -3 to 3
- slowness: float32 [256, 4, 1024], P(('group', 'tile')), parts along dimension 0, may hold values from -1 to 1
Outputs:
- gradient: float32 [256, 4, 1024], P(('group', 'tile')), parts along dimension 0
There are 2 independent parts, one for each index of `group`. A program takes and returns all parts, laid end to end along the dimension named above; an argument that names none is the same for every part. Nothing has to cross between parts.
Inputs may be any that keep to these rules, and one draw needn't show every extreme that they name: `tile_at`: A permutation of the 128 tile numbers; in every window (tile columns b * 8 to b * 8 + 7) each value of t // 8 that occurs there occurs for exactly 4 tiles.
All inputs are finite; a program needn't handle non-finite values.
Results may differ from a plain program's by a relative error of at most 0.0003.
Values sent between devices are 32-bit elements; how exact they have to be, the bound alone decides.
A program may use at most 64 MiB of HBM per device.

v0:
```python
import functools
import math

import jax
import jax.numpy as jnp
import numpy as np
from jax import lax
from jax.experimental import pallas as pl
from jax.experimental.pallas import tpu as pltpu
from jax.sharding import PartitionSpec as P

A = 256
TL = 32
SIDE = A // TL
CELLS = SIDE * SIDE
SECTIONS = 4
NZ = 4
NF = 2
NFT = 600
ROWS = A // SECTIONS
LENS_GAIN = 3.0
VMEM_LIMIT = 56 * 1024 * 1024

F32 = jnp.float32
BF16 = jnp.bfloat16


def sin_cos(angle):
    t = angle * 0.5
    u = t * t
    s = -1.0 / math.factorial(11)
    for n in (9, 7, 5, 3, 1):
        s = s * u + (-1.0) ** (n // 2) / math.factorial(n)
    s = s * t
    c = 1.0 / math.factorial(12)
    for n in (10, 8, 6, 4, 2, 0):
        c = c * u + (-1.0) ** (n // 2) / math.factorial(n)
    return 2.0 * s * c, 1.0 - 2.0 * s * s


def split(values):
    high = values.astype(BF16)
    return high, (values - high.astype(F32)).astype(BF16)


def dot(a, b):
    return lax.dot_general(a, b, (((1,), (0,)), ((), ())), preferred_element_type=F32)


def split_dot_left(op_high, op_low, values):
    high, low = split(values)
    return dot(op_high, high) + dot(op_high, low) + dot(op_low, high)


def split_dot_right(values, op_high, op_low):
    high, low = split(values)
    return dot(high, op_high) + dot(high, op_low) + dot(low, op_high)


def swap_groups(tiles):
    lane = lax.broadcasted_iota(jnp.int32, tiles[0].shape, tiles[0].ndim - 1)
    axis = tiles[0].ndim - 1

    def exchange(low, high, width, first):
        return (
            jnp.where(first, low, pltpu.roll(high, width, axis)),
            jnp.where(first, pltpu.roll(low, 128 - width, axis), high),
        )

    first = lane < 64
    a0, a2 = exchange(tiles[0], tiles[2], 64, first)
    a1, a3 = exchange(tiles[1], tiles[3], 64, first)
    first = (lane & 32) == 0
    b0, b1 = exchange(a0, a1, 32, first)
    b2, b3 = exchange(a2, a3, 32, first)
    return b0, b1, b2, b3


def greet_all(me, count):
    barrier = pltpu.get_barrier_semaphore()

    def signal(step, carry):
        pl.semaphore_signal(
            barrier,
            inc=1,
            device_id={"tile": lax.rem(me + step, count)},
            device_id_type=pl.DeviceIdType.MESH,
        )
        return carry

    lax.fori_loop(1, count, signal, 0)
    pl.semaphore_wait(barrier, count - 1)


def remote(src, dst, send_sem, recv_sem, target):
    return pltpu.make_async_remote_copy(
        src_ref=src,
        dst_ref=dst,
        send_sem=send_sem,
        recv_sem=recv_sem,
        device_id={"tile": target},
        device_id_type=pl.DeviceIdType.MESH,
    )


def scatter_kernel(
    count, cap, picks, model, observed, got_model, got_rows, packed, send_sem, recv_sem, row_send, row_recv, local_sem
):
    me = lax.axis_index("tile")
    shots = count // SECTIONS
    pairs = shots * NF
    pair = me // 2
    computes = lax.rem(me, 2) == 0
    section, column = me // shots, lax.rem(me, shots)
    greet_all(me, count)

    def rows_copy(freq):
        return remote(
            observed.at[freq], got_rows.at[section], row_send.at[freq], row_recv.at[section], 2 * (NF * column + freq)
        )

    for freq in range(NF):
        there = 2 * (NF * column + freq)

        @pl.when(there != me)
        def _():
            rows_copy(freq).start()

        @pl.when(there == me)
        def _():
            keep = pltpu.make_async_copy(observed.at[freq], got_rows.at[section], local_sem)
            keep.start()
            keep.wait()

    def pack(slot, carry):
        packed[slot] = model[picks[slot]]
        return carry

    lax.fori_loop(0, shots * cap, pack, 0)

    def model_copy(to):
        return remote(
            packed.at[pl.ds((to // NF) * cap, cap)],
            got_model.at[pl.ds(me * cap, cap)],
            send_sem.at[to],
            recv_sem.at[me],
            2 * to,
        )

    def send(step, carry):
        to = lax.rem(pair + step, pairs)

        @pl.when(2 * to != me)
        def _():
            model_copy(to).start()

        @pl.when(2 * to == me)
        def _():
            keep = pltpu.make_async_copy(
                packed.at[pl.ds((to // NF) * cap, cap)], got_model.at[pl.ds(me * cap, cap)], local_sem
            )
            keep.start()
            keep.wait()

        return carry

    lax.fori_loop(0, pairs, send, 0)

    @pl.when(computes)
    def _():
        def arrive(step, carry):
            source = lax.rem(me + step, count)
            remote(
                packed.at[pl.ds(0, cap)], got_model.at[pl.ds(source * cap, cap)], send_sem.at[0], recv_sem.at[source], source
            ).wait_recv()
            return carry

        lax.fori_loop(1, count, arrive, 0)
        for part in range(SECTIONS):

            @pl.when(part * shots + pair // NF != me)
            def _():
                remote(observed.at[0], got_rows.at[part], row_send.at[0], row_recv.at[part], me + 1).wait_recv()

    def sent(to, carry):
        @pl.when(2 * to != me)
        def _():
            model_copy(to).wait_send()

        return carry

    lax.fori_loop(0, pairs, sent, 0)
    for freq in range(NF):

        @pl.when(2 * (NF * column + freq) != me)
        def _():
            rows_copy(freq).wait_send()


def march_kernel(
    numbers,
    window_slot,
    angular_ref,
    phase,
    table_cos,
    table_sin,
    model,
    rows,
    tiles_out,
    slow,
    reflect,
    lens,
    fields,
    spare,
    left_ops,
    right_ops,
):
    @pl.when(numbers[0] == 1)
    def _():
        angular = angular_ref[0]
        s, c = sin_cos(jnp.broadcast_to(phase[...], (8, A)))

        def table_dot(a, b):
            return lax.dot_general(
                a, b, (((1,), (0,)), ((), ())), preferred_element_type=F32, precision=lax.Precision.HIGHEST
            )

        c_cos, c_sin = table_dot(c, table_cos[...]), table_dot(c, table_sin[...])
        s_cos, s_sin = table_dot(s, table_cos[...]), table_dot(s, table_sin[...])
        scale = 1.0 / A

        def turned(row):
            return pltpu.roll(jnp.broadcast_to(row[0:1], (A, A)), 0, 1, stride=1, stride_axis=0)

        o_re, o_im = turned((c_cos + s_sin) * scale), turned((s_cos - c_sin) * scale)
        t_re, t_im = turned((c_cos - s_sin) * scale), turned((s_cos + c_sin) * scale)

        def put(ref, which, blocks):
            for i, block in enumerate(blocks):
                high, low = split(block)
                at = (pl.ds((i // 2) * A, A), pl.ds((i % 2) * A, A))
                ref[(2 * which, *at)] = high
                ref[(2 * which + 1, *at)] = low

        put(left_ops, 0, (o_re, -o_im, o_im, o_re))
        put(left_ops, 1, (t_re, t_im, -t_im, t_re))
        put(right_ops, 0, (t_re, t_im, -t_im, t_re))
        put(right_ops, 1, (o_re, -o_im, o_im, o_re))

        def gather(block_row, carry):
            for half in range(SIDE // 4):
                tiles = [model[window_slot[block_row * SIDE + half * 4 + j]] for j in range(4)]
                for k, part in enumerate(swap_groups(tiles)):
                    at = (half, pl.ds(block_row * TL + k, 8, stride=4))
                    for z in range(NZ):
                        reflect[(z, *at)] = part[z]
                        slow[(z, *at)] = part[NZ + z]
            return carry

        lax.fori_loop(0, SIDE, gather, 0)

        def whole(ref, z):
            return jnp.concatenate([ref[z, 0], ref[z, 1]], axis=1)

        def make_lens(z, carry):
            s, c = sin_cos(whole(slow, z) * (LENS_GAIN * angular))
            lens[z, 0] = c
            lens[z, 1] = s
            return carry

        lax.fori_loop(0, NZ, make_lens, 0)

        def extend(z, re, im):
            c, s = lens[z, 0], lens[z, 1]
            stacked = jnp.concatenate([c * re - s * im, c * im + s * re], axis=0)
            left = split_dot_left(left_ops[0], left_ops[1], stacked)
            beside = jnp.concatenate([left[:A], left[A:]], axis=1)
            right = split_dot_right(beside, right_ops[0], right_ops[1])
            return right[:, :A], right[:, A:]

        row_id = lax.broadcasted_iota(jnp.int32, (A, A), 0)
        column_id = lax.broadcasted_iota(jnp.int32, (A, A), 1)
        spike = jnp.where((row_id == numbers[1]) & (column_id == numbers[2]), float(A), 0.0).astype(F32)
        spare[0] = spike
        spare[1] = jnp.zeros((A, A), F32)

        def down(z, carry):
            re, im = extend(z, spare[0], spare[1])
            spare[0] = re
            spare[1] = im
            fields[z, 0] = re
            fields[z, 1] = im
            return carry

        lax.fori_loop(0, NZ, down, 0)
        spare[...] = jnp.zeros_like(spare)

        def up(step, carry):
            z = NZ - 1 - step
            weight = whole(reflect, z) * angular
            re, im = extend(z, spare[0] - weight * fields[z, 1], spare[1] + weight * fields[z, 0])
            spare[0] = re
            spare[1] = im
            return carry

        lax.fori_loop(0, NZ, up, 0)
        for part in range(SECTIONS):
            for half in range(2):
                at = (half, pl.ds(part * ROWS, ROWS))
                spare[at] = spare[at] - rows[part, half]

        def back(z, carry):
            left = split_dot_left(left_ops[2], left_ops[3], jnp.concatenate([spare[0], spare[1]], axis=0))
            beside = jnp.concatenate([left[:A], left[A:]], axis=1)
            right = split_dot_right(beside, right_ops[2], right_ops[3])
            re, im = right[:, :A], right[:, A:]
            c, s = lens[z, 0], lens[z, 1]
            re, im = c * re + s * im, c * im - s * re
            spare[0] = re
            spare[1] = im
            partial = angular * (im * fields[z, 0] - re * fields[z, 1])
            slow[z, 0] = partial[:, :128]
            slow[z, 1] = partial[:, 128:]
            return carry

        lax.fori_loop(0, NZ, back, 0)

        def give(block_row, carry):
            for half in range(SIDE // 4):
                parts = []
                for k in range(4):
                    at = (half, pl.ds(block_row * TL + k, 8, stride=4))
                    parts.append(jnp.stack([slow[(z, *at)] for z in range(NZ)]))
                for j, tile in enumerate(swap_groups(parts)):
                    tiles_out[block_row * SIDE + half * 4 + j] = tile
            return carry

        lax.fori_loop(0, SIDE, give, 0)


def return_kernel(
    count, cap, places, owned, ranks, homes, blocks, tiles, out, got, packed, send_sem, recv_sem, local_sem
):
    me = lax.axis_index("tile")
    shots = count // SECTIONS
    pairs = shots * NF
    pair = me // 2
    computes = lax.rem(me, 2) == 0
    greet_all(me, count)

    def tile_copy(to):
        return remote(packed.at[to], got.at[pair], send_sem.at[to], recv_sem.at[pair], to)

    @pl.when(computes)
    def _():
        def send(step, carry):
            to = lax.rem(me + step, count)
            for slot in range(cap):
                packed[to, slot] = tiles[places[to * cap + slot]]

            @pl.when(to != me)
            def _():
                tile_copy(to).start()

            @pl.when(to == me)
            def _():
                keep = pltpu.make_async_copy(packed.at[to], got.at[pair], local_sem)
                keep.start()
                keep.wait()

            return carry

        lax.fori_loop(0, count, send, 0)

    def arrive(source, carry):
        @pl.when(2 * source != me)
        def _():
            remote(packed.at[0], got.at[source], send_sem.at[0], recv_sem.at[source], 2 * source).wait_recv()

        return carry

    lax.fori_loop(0, pairs, arrive, 0)
    for tile in range(owned):

        def add(source, total):
            mine = homes[tile] == blocks[source // NF]
            return total + jnp.where(mine, got[source, ranks[tile]], 0.0)

        out[tile] = lax.fori_loop(0, pairs, add, jnp.zeros((NZ, 8, 128), F32))

    @pl.when(computes)
    def _():
        def sent(step, carry):
            tile_copy(lax.rem(me + step, count)).wait_send()
            return carry

        lax.fori_loop(1, count, sent, 0)


def total_of(values, axis):
    return jnp.sum(values, axis=axis, dtype=jnp.int32)


def shards(wave_phase, tile_at, aperture_block, source_cell, freq_index, observed, image, slowness):
    count = lax.axis_size("tile")
    me = lax.axis_index("tile")
    owned = image.shape[0]
    shots = count // SECTIONS
    pairs = shots * NF
    cap = max(1, CELLS // count)
    pair = me // 2
    shot, freq = pair // NF, pair % NF

    my_ids = me * owned + jnp.arange(owned, dtype=jnp.int32)
    matches = (tile_at[None] == my_ids[:, None, None]).astype(jnp.int32)
    place_row = jnp.arange(tile_at.shape[0], dtype=jnp.int32)[None, :, None]
    place_column = jnp.arange(tile_at.shape[1], dtype=jnp.int32)[None, None, :]
    spot = place_column // SIDE * CELLS + place_row * SIDE + place_column % SIDE
    spots = total_of(matches * spot, (1, 2))
    homes = spots // CELLS
    earlier = (homes[:, None] == homes[None, :]) & (spots[None, :] < spots[:, None])
    ranks = total_of(earlier, 1)
    slot_id = jnp.arange(shots * cap, dtype=jnp.int32)
    wanted = aperture_block[slot_id // cap]
    picks = total_of(
        ((homes[None, :] == wanted[:, None]) & (ranks[None, :] == (slot_id % cap)[:, None])).astype(jnp.int32)
        * jnp.arange(owned, dtype=jnp.int32)[None, :],
        1,
    )

    block = aperture_block[shot]
    window_ids = lax.dynamic_slice(tile_at, (jnp.int32(0), block * SIDE), (SIDE, SIDE)).reshape(CELLS)
    owners = window_ids // owned
    order = jnp.arange(CELLS, dtype=jnp.int32)
    before = (owners[:, None] == owners[None, :]) & (order[None, :] < order[:, None])
    window_slot = owners * cap + total_of(before, 1)
    places = total_of(
        (window_slot[None, :] == jnp.arange(count * cap, dtype=jnp.int32)[:, None]).astype(jnp.int32) * order[None, :], 1
    )

    chosen = freq_index[shot, freq]
    angular = ((chosen + 1).astype(F32) / NFT).reshape(1)
    phase = lax.dynamic_slice(wave_phase, (chosen, jnp.int32(0)), (1, A))
    numbers = jnp.stack([(me % 2 == 0).astype(jnp.int32), source_cell[shot, 0], source_cell[shot, 1]])
    turns = 2.0 * np.pi / A * (np.outer(np.arange(A), np.arange(A)) % A)
    table_cos = jnp.asarray(np.cos(turns), F32)
    table_sin = jnp.asarray(np.sin(turns), F32)

    model = jnp.concatenate([image, slowness], axis=1).reshape(owned, 2 * NZ, 8, 128)
    smem = pl.BlockSpec(memory_space=pltpu.SMEM)
    vmem = pl.BlockSpec(memory_space=pltpu.VMEM)

    got_model, got_rows = pl.pallas_call(
        functools.partial(scatter_kernel, count, cap),
        out_shape=(
            jax.ShapeDtypeStruct((count * cap, 2 * NZ, 8, 128), F32),
            jax.ShapeDtypeStruct((SECTIONS, 2, ROWS, A), F32),
        ),
        in_specs=[smem, vmem, vmem],
        out_specs=(vmem, vmem),
        scratch_shapes=[
            pltpu.VMEM((shots * cap, 2 * NZ, 8, 128), F32),
            pltpu.SemaphoreType.DMA((pairs,)),
            pltpu.SemaphoreType.DMA((count,)),
            pltpu.SemaphoreType.DMA((NF,)),
            pltpu.SemaphoreType.DMA((SECTIONS,)),
            pltpu.SemaphoreType.DMA,
        ],
        compiler_params=pltpu.CompilerParams(collective_id=0, has_side_effects=True, vmem_limit_bytes=VMEM_LIMIT),
    )(picks, model, observed[0])

    tiles = pl.pallas_call(
        march_kernel,
        out_shape=jax.ShapeDtypeStruct((CELLS, NZ, 8, 128), F32),
        in_specs=[smem, smem, smem, vmem, vmem, vmem, vmem, vmem],
        out_specs=vmem,
        scratch_shapes=[
            pltpu.VMEM((NZ, 2, A, 128), F32),
            pltpu.VMEM((NZ, 2, A, 128), F32),
            pltpu.VMEM((NZ, 2, A, A), F32),
            pltpu.VMEM((NZ, 2, A, A), F32),
            pltpu.VMEM((2, A, A), F32),
            pltpu.VMEM((4, 2 * A, 2 * A), BF16),
            pltpu.VMEM((4, 2 * A, 2 * A), BF16),
        ],
        compiler_params=pltpu.CompilerParams(vmem_limit_bytes=VMEM_LIMIT),
    )(numbers, window_slot, angular, phase, table_cos, table_sin, got_model, got_rows)

    out = pl.pallas_call(


        (lambda places, ranks, homes, blocks, *rest: return_kernel(count, cap, places, owned, ranks, homes, blocks, *rest)),
        out_shape=jax.ShapeDtypeStruct((owned, NZ, 8, 128), F32),
        in_specs=[smem, smem, smem, smem, vmem],
        out_specs=vmem,
        scratch_shapes=[
            pltpu.VMEM((pairs, cap, NZ, 8, 128), F32),
            pltpu.VMEM((count, cap, NZ, 8, 128), F32),
            pltpu.SemaphoreType.DMA((count,)),
            pltpu.SemaphoreType.DMA((pairs,)),
            pltpu.SemaphoreType.DMA,
        ],
        compiler_params=pltpu.CompilerParams(collective_id=1, has_side_effects=True, vmem_limit_bytes=VMEM_LIMIT),
    )(places, ranks, homes, aperture_block, tiles)
    return out.reshape(owned, NZ, TL * TL)


def solution(mesh):
    return jax.shard_map(
        shards,
        mesh=mesh,
        in_specs=(
            P(),
            P(),
            P("group"),
            P("group", None),
            P("group", None),
            P(("group", "tile"), None, None, None, None),
            P(("group", "tile"), None, None),
            P(("group", "tile"), None, None),
        ),
        out_specs=P(("group", "tile"), None, None),
        check_vma=False,
    )
```

profile of v0, /device:TPU:15, one launch (start us, length us, event | category | flops | bytes accessed | tf_op | source)
XLA Modules:
  0.0 111.3 jit_solution(17506325416136397254)
XLA Ops:
  0.0 0.0 copy-start
  0.0 1.4 %dynamic_slice.22 = s32[1,1]{0,1:T(1,128)} dynamic-slice(s32[4,2]{0,1:T(2,128)} %param.14, s32[]{:T(128)S(6)} %select_n.109, s32[]{:T(128)S(6)} %select_n.117), dynamic_slice_sizes={1,1} | dynamic-slice | bytes 12 | tf_op jit(solution)/shard_map/dynamic_slice | solution.py:441
  3.5 0.0 copy-done
  3.5 0.6 constant_dynamic-slice_fusion.phase
  4.8 1.4 %constant_dynamic-slice_fusion.1 = (s32[1,1]{0,1:T(1,128)}, s32[1,1]{0,1:T(1,128)}) fusion(s32[4,2]{0,1:T(2,128)} %param.13, s32[]{:T(128)S(6)} %select_n.109), kind=kLoop, calls=%fused_computation.33 | loop fusion | bytes 20 | tf_op jit(solution)/shard_map/dynamic_slice | solution.py:444
  6.2 1.9 %pad_add_fusion.numbers = s32[3]{0:T(128)} fusion(s32[1]{0:T(128)} %bitcast.3, s32[1]{0:T(128)} %bitcast.2, s32[1]{0:T(128)} %bitcast.1), kind=kLoop, calls=%fused_computation.37 | loop fusion | flops 6 | bytes 24 | tf_op jit(solution)/shard_map/stack | solution.py:444
  8.1 1.3 %dynamic_slice.18 = s32[1]{0:T(128)} dynamic-slice(s32[4]{0:T(128)} %blocks.1, s32[]{:T(128)S(6)} %select_n.109), dynamic_slice_sizes={1} | dynamic-slice | bytes 12 | tf_op jit(solution)/shard_map/dynamic_slice | solution.py:431
  10.1 0.8 constant_dynamic-slice_fusion.2
  10.9 0.1 reshape.287
  11.0 0.2 convert_reduce_fusion
  11.2 0.6 multiply_add_fusion.window_slot
  11.8 0.1 add_add_fusion
  11.9 1.0 select_reduce_fusion
  12.9 0.0 copy-start.1
  12.9 0.2 convert_reduce_fusion.1.ranks
  13.1 0.0 copy-start.2
  13.1 1.3 %gather_fusion = s32[16]{0:T(128)S(1)} fusion(s32[4]{0:T(128)} %blocks.1, s32[1024]{0:T(1024)S(1)} %pad_clamp_fusion), kind=kCustom, calls=%fused_computation | custom fusion | bytes 192 | tf_op jit(solution)/shard_map/gather | solution.py:424
  14.4 0.6 select_reduce_fusion.2.picks
  15.0 1.0 maximum_bitcast_fusion
  16.0 0.8 copy.13
  16.8 40.1 %shard_map.100 = (f32[64,8,8,128]{3,2,1,0:T(8,128)}, f32[4,2,64,256]{3,2,1,0:T(8,128)}) custom-call(s32[16]{0:T(128)} %select_reduce_fusion.2.picks, f32[8,8,8,128]{3,2,1,0:T(8,128)} %copy.13, f32[2,2,64,256]{3,2,1,0:T(8,128)} %bitcast.18), custom_call_target="tpu_custom_call" | custom-call | tf_op jit(solution)/shard_map/pallas_call | solution.py:453
  56.9 0.0 copy-start.3
  56.9 2.9 %shard_map.101.rest_0_ = f32[64,4,8,128]{3,2,1,0:T(8,128)} custom-call(s32[3]{0:T(128)} %pad_add_fusion.numbers, s32[64]{0:T(128)} %multiply_add_fusion.window_slot, f32[1]{0:T(128)} %bitcast.5.angular_ref, f32[1,256]{1,0:T(1,128)} %constant_dynamic-slice_fusion.phase, f32[256,256]{1,0:T(8,128)} %constant.139.clone.table_cos, ...), custom_call_target="tpu_custom_call" | custom-call | tf_op jit(solution)/shard_map/pallas_call | solution.py:472
  59.8 0.0 copy-done.1
  59.8 0.0 copy-done.2
  59.8 0.0 copy-done.3
  59.8 0.6 select_reduce_fusion.1.places
  60.4 49.2 %shard_map.102 = f32[8,4,8,128]{3,2,1,0:T(8,128)} custom-call(s32[64]{0:T(128)} %select_reduce_fusion.1.places, s32[8]{0:T(128)} %copy-done.2, s32[8]{0:T(128)} %copy-done.1, s32[4]{0:T(128)} %blocks.1, f32[64,4,8,128]{3,2,1,0:T(8,128)} %shard_map.101.rest_0_), custom_call_target="tpu_custom_call" | custom-call | tf_op jit(solution)/shard_map/pallas_call | solution.py:489
  109.6 1.6 %reshape.290 = f32[8,4,1024]{2,1,0:T(4,128)} reshape(f32[8,4,8,128]{3,2,1,0:T(8,128)} %shard_map.102) | data formatting | bytes 262144 | tf_op jit(solution)/shard_map/reshape | solution.py:505
  (8 shorter events, 0.1 us)
Async XLA Ops:
  0.0 3.5 %copy-start = (f32[600,256]{1,0:T(8,128)S(1)}, f32[600,256]{1,0:T(8,128)}, u32[]{:S(2)}) copy-start(f32[600,256]{1,0:T(8,128)} %param.10) | copy-start | bytes 1843204
  12.9 46.9 %copy-start.1 = (s32[8]{0:T(128)}, s32[8]{0:T(128)S(1)}, u32[]{:S(2)}) copy-start(s32[8]{0:T(128)S(1)} %and_select_fusion.2.homes) | copy-start | bytes 100
  13.1 46.7 %copy-start.2 = (s32[8]{0:T(128)}, s32[8]{0:T(128)S(1)}, u32[]{:S(2)}) copy-start(s32[8]{0:T(128)S(1)} %convert_reduce_fusion.1.ranks) | copy-start | bytes 100
  56.9 2.9 %copy-start.3 = (s32[64]{0:T(128)S(1)}, s32[64]{0:T(128)}, u32[]{:S(2)}) copy-start(s32[64]{0:T(128)} %multiply_add_fusion.window_slot) | copy-start | bytes 772
where the time goes:
time: 112 us; the launch traced here: 111 us
  Pallas kernels  92.2 us (82%)
  local copies, waits for them, and re-layouts  9.27 us (8%)
  other arithmetic  6.23 us (6%)
  between operations  3.57 us (3%)
    pallas_call x1, Pallas kernels, shards(): pl.pallas_call(lambda places, ranks, homes, blocks, *rest: return_kernel(...  49.2 us
    pallas_call x1, Pallas kernels, shards(): pl.pallas_call(functools.partial(scatter_kernel, count, cap), out_shape=(...  40.1 us
    pallas_call x1, Pallas kernels, shards(): pl.pallas_call(march_kernel, out_shape=jax.ShapeDtypeStruct((CELLS, NZ, 8...  2.86 us
    reduce_sum x5, other arithmetic, total_of(): return jnp.sum(values, axis=axis, dtype=jnp.int32)  2.57 us

commit v1 on v0

v1 whole, which is shorter than its diff:
```python
import functools
import math

import jax
import jax.numpy as jnp
import numpy as np
from jax import lax
from jax.experimental import pallas as pl
from jax.experimental.pallas import tpu as pltpu
from jax.sharding import PartitionSpec as P

A = 256
TL = 32
SIDE = A // TL
CELLS = SIDE * SIDE
SECTIONS = 4
NZ = 4
NF = 2
NFT = 600
ROWS = A // SECTIONS
LENS_GAIN = 3.0
VMEM_LIMIT = 56 * 1024 * 1024

F32 = jnp.float32
BF16 = jnp.bfloat16


def sin_cos(angle):
    t = angle * 0.5
    u = t * t
    s = -1.0 / math.factorial(11)
    for n in (9, 7, 5, 3, 1):
        s = s * u + (-1.0) ** (n // 2) / math.factorial(n)
    s = s * t
    c = 1.0 / math.factorial(12)
    for n in (10, 8, 6, 4, 2, 0):
        c = c * u + (-1.0) ** (n // 2) / math.factorial(n)
    return 2.0 * s * c, 1.0 - 2.0 * s * s


def split(values):
    high = values.astype(BF16)
    return high, (values - high.astype(F32)).astype(BF16)


def dot(a, b):
    return lax.dot_general(a, b, (((1,), (0,)), ((), ())), preferred_element_type=F32)


def swap_groups(tiles):
    lane = lax.broadcasted_iota(jnp.int32, tiles[0].shape, tiles[0].ndim - 1)
    axis = tiles[0].ndim - 1

    def exchange(low, high, width, first):
        return (
            jnp.where(first, low, pltpu.roll(high, width, axis)),
            jnp.where(first, pltpu.roll(low, 128 - width, axis), high),
        )

    first = lane < 64
    a0, a2 = exchange(tiles[0], tiles[2], 64, first)
    a1, a3 = exchange(tiles[1], tiles[3], 64, first)
    first = (lane & 32) == 0
    b0, b1 = exchange(a0, a1, 32, first)
    b2, b3 = exchange(a2, a3, 32, first)
    return b0, b1, b2, b3


def greet_all(me, count):
    barrier = pltpu.get_barrier_semaphore()

    def signal(step, carry):
        pl.semaphore_signal(
            barrier,
            inc=1,
            device_id={"tile": lax.rem(me + step, count)},
            device_id_type=pl.DeviceIdType.MESH,
        )
        return carry

    lax.fori_loop(1, count, signal, 0)
    pl.semaphore_wait(barrier, count - 1)


def remote(src, dst, send_sem, recv_sem, target):
    return pltpu.make_async_remote_copy(
        src_ref=src,
        dst_ref=dst,
        send_sem=send_sem,
        recv_sem=recv_sem,
        device_id={"tile": target},
        device_id_type=pl.DeviceIdType.MESH,
    )


def index_kernel(count, cap, owned, tile_at, blocks, source_cell, freq_index, wave_phase,
                 picks, window_slot, places, homes, ranks, numbers, angular, phase, own_at, seen, rows, sem):
    me = lax.axis_index("tile")
    shots = count // SECTIONS
    shot = jnp.clip(lax.div(me, 2) - shots // 2, 0, shots - 1)
    chosen = freq_index[shot, lax.rem(me, 2)]
    first = lax.div(chosen, 8) * 8
    fetch = pltpu.make_async_copy(wave_phase.at[pl.ds(pl.multiple_of(first, 8), 8)], rows, sem)
    fetch.start()
    windows = tile_at.shape[1] // SIDE

    def clear(ref, size):
        def one(i, carry):
            ref[i] = 0
            return carry

        lax.fori_loop(0, size, one, 0)

    clear(own_at, windows * cap)
    clear(seen, count)
    clear(places, count * cap)

    def spot(window, place):
        return tile_at[lax.div(place, SIDE), window * SIDE + lax.rem(place, SIDE)]

    def in_window(window, carry):
        def look(place, rank):
            mine = spot(window, place) - me * owned
            held = (mine >= 0) & (mine < owned)

            @pl.when(held)
            def _():
                homes[mine] = window
                ranks[mine] = rank
                own_at[window * cap + rank] = mine

            return rank + held.astype(jnp.int32)

        lax.fori_loop(0, CELLS, look, 0)
        return carry

    lax.fori_loop(0, windows, in_window, 0)

    def pick(slot, carry):
        picks[slot] = own_at[blocks[lax.div(slot, cap)] * cap + lax.rem(slot, cap)]
        return carry

    lax.fori_loop(0, shots * cap, pick, 0)
    window = blocks[shot]

    def order(place, carry):
        owner = lax.div(spot(window, place), owned)
        rank = seen[owner]
        seen[owner] = rank + 1
        window_slot[place] = owner * cap + rank
        places[owner * cap + rank] = place
        return carry

    lax.fori_loop(0, CELLS, order, 0)
    numbers[0] = source_cell[shot, 0]
    numbers[1] = source_cell[shot, 1]
    angular[0] = (chosen + 1).astype(F32) / NFT
    fetch.wait()
    phase[...] = rows[pl.ds(lax.rem(chosen, 8), 1)]


def whole(ref, *at):
    return jnp.concatenate([ref[(*at, 0)], ref[(*at, 1)]], axis=1)


def build_operators(phase, table_cos, table_sin, left_ops, right_ops):
    s, c = sin_cos(jnp.broadcast_to(phase[...], (8, A)))

    def table_dot(a, b):
        return lax.dot_general(
            a, b, (((1,), (0,)), ((), ())), preferred_element_type=F32, precision=lax.Precision.HIGHEST
        )

    c_cos, c_sin = table_dot(c, table_cos[...]), table_dot(c, table_sin[...])
    s_cos, s_sin = table_dot(s, table_cos[...]), table_dot(s, table_sin[...])
    scale = 1.0 / A

    def turned(row):
        return pltpu.roll(jnp.broadcast_to(row[0:1], (A, A)), 0, 1, stride=1, stride_axis=0)

    o_re, o_im = turned((c_cos + s_sin) * scale), turned((s_cos - c_sin) * scale)
    t_re, t_im = turned((c_cos - s_sin) * scale), turned((s_cos + c_sin) * scale)

    def put(ref, which, blocks, left):
        for i, block in enumerate(blocks):
            high, low = split(block)
            for third, part in enumerate((high, high, low)):
                a, b = (i // 2) * A, (i % 2) * A
                if left:
                    ref[which, pl.ds(a, A), pl.ds(third * 2 * A + b, A)] = part
                else:
                    ref[which, pl.ds(third * 2 * A + a, A), pl.ds(b, A)] = part

    put(left_ops, 0, (o_re, -o_im, o_im, o_re), True)
    put(left_ops, 1, (t_re, t_im, -t_im, t_re), True)
    put(right_ops, 0, (t_re, t_im, -t_im, t_re), False)
    put(right_ops, 1, (o_re, -o_im, o_im, o_re), False)


def both_sides(left_ops, right_ops, which, re, im):
    high, low = split(jnp.concatenate([re, im], axis=0))
    left = dot(left_ops[which], jnp.concatenate([high, low, high], axis=0))
    high, low = split(jnp.concatenate([left[:A], left[A:]], axis=1))
    right = dot(jnp.concatenate([high, low, high], axis=1), right_ops[which])
    return right[:, :A], right[:, A:]


def gather(got, window_slot, cells):
    def one(block_row, carry):
        for half in range(SIDE // 4):
            slots = [window_slot[block_row * SIDE + half * 4 + j] for j in range(4)]
            for z in range(NZ):
                tiles = [got[slot, pl.ds(z, 8, stride=NZ)] for slot in slots]
                for k, part in enumerate(swap_groups(tiles)):
                    cells[z, half, pl.ds(block_row * TL + k, 8, stride=4)] = part
        return carry

    lax.fori_loop(0, SIDE, one, 0)


def migrate_kernel(
    count, cap, owned,
    picks, window_slot, places, homes, ranks, numbers, angular_ref, blocks,
    phase, table_cos, table_sin, image, slowness, observed,
    out,
    packed, got_slow, got_image, rows, cells, reflect, partial, lens, fields, spare, left_ops, right_ops,
    tiles, half_sums, sibling_sums, sums, got_sums,
    send_sem, recv_sem, forward_sem, row_send, row_recv, swap_send, swap_recv, sum_send, sum_recv,
):
    me = lax.axis_index("tile")
    got = (got_slow, got_image)
    shots = count // SECTIONS
    chip, core = lax.div(me, 2), lax.rem(me, 2)
    shot = chip - shots // 2
    computes = (shot >= 0) & (shot < shots)
    sibling = me + 1 - 2 * core
    section, column = lax.div(me, shots), lax.rem(me, shots)

    def marcher(shot_id, freq):
        return 2 * (shot_id + shots // 2) + freq

    greet_all(me, count)

    def pack(slot, carry):
        tile = picks[slot]
        for kind, source in enumerate((slowness, image)):
            levels = source[tile]
            for chunk in range(8):
                packed[kind, slot, pl.ds(chunk * NZ, NZ)] = levels[:, chunk * 128 : chunk * 128 + 128]
        return carry

    lax.fori_loop(0, shots * cap, pack, 0)

    def model_copy(kind, to):
        return remote(
            packed.at[kind, pl.ds(to * cap, cap)],
            got[kind].at[pl.ds(me * cap, cap)],
            send_sem.at[kind, to],
            recv_sem.at[kind, me],
            marcher(to, core),
        )

    def send_model(kind):
        def send(step, carry):
            to = lax.rem(column + step, shots)

            @pl.when(marcher(to, core) != me)
            def _():
                model_copy(kind, to).start()

            @pl.when(marcher(to, core) == me)
            def _():
                for slot in range(cap):
                    got[kind][me * cap + slot] = packed[kind, to * cap + slot]

            return carry

        lax.fori_loop(0, shots, send, 0)

    def rows_copy(freq):
        return remote(
            observed.at[0, freq], rows.at[section], row_send.at[freq], row_recv.at[section], marcher(column, freq)
        )

    send_model(0)
    send_model(1)
    for freq in range(NF):

        @pl.when(marcher(column, freq) != me)
        def _():
            rows_copy(freq).start()

        @pl.when(marcher(column, freq) == me)
        def _():
            rows[section] = observed[0, freq]

    def forward_copy(kind, step):
        source = lax.rem(me + 2 * step, count)
        block = got[kind].at[pl.ds(source * cap, cap)]
        return remote(block, block, forward_sem.at[kind, step], recv_sem.at[kind, source], sibling)

    def arrival(kind, source):
        return remote(
            packed.at[kind, pl.ds(0, cap)],
            got[kind].at[pl.ds(source * cap, cap)],
            send_sem.at[kind, 0],
            recv_sem.at[kind, source],
            sibling,
        )

    def forward(kind):
        forward_copy(kind, 0).start()

        def one(step, carry):
            arrival(kind, lax.rem(me + 2 * step, count)).wait_recv()
            forward_copy(kind, step).start()
            return carry

        lax.fori_loop(1, count // 2, one, 0)

    def arrive(kind):
        def one(step, carry):
            arrival(kind, lax.rem(sibling + 2 * step, count)).wait_recv()
            return carry

        lax.fori_loop(0, count // 2, one, 0)

    def swap_copy(z):
        return remote(half_sums.at[z, 1 - core], sibling_sums.at[z], swap_send.at[z], swap_recv.at[z], sibling)

    def sum_copy(z, step):
        owner = lax.rem(me + 2 * step, count)
        return remote(
            sums.at[z, lax.div(owner, 2)], got_sums.at[z, shot], sum_send.at[z, step], sum_recv.at[z, shot], owner
        )

    def finish_level(z):
        swap_copy(z).wait_recv()
        sums[z] = half_sums[z, core] + sibling_sums[z]

        def one(step, carry):
            sum_copy(z, step).start()
            return carry

        lax.fori_loop(1, count // 2, one, 0)
        got_sums[z, shot] = sums[z, lax.div(me, 2)]

    @pl.when(computes)
    def _():
        angular = angular_ref[0]
        build_operators(phase, table_cos, table_sin, left_ops, right_ops)
        row_id = lax.broadcasted_iota(jnp.int32, (A, A), 0)
        column_id = lax.broadcasted_iota(jnp.int32, (A, A), 1)
        spare[0] = jnp.where((row_id == numbers[0]) & (column_id == numbers[1]), float(A), 0.0).astype(F32)
        spare[1] = jnp.zeros((A, A), F32)
        forward(0)
        arrive(0)
        gather(got[0], window_slot, cells)

        def extend(z, re, im):
            c, s = lens[z, 0], lens[z, 1]
            return both_sides(left_ops, right_ops, 0, c * re - s * im, c * im + s * re)

        def down(z, carry):
            s, c = sin_cos(whole(cells, z) * (LENS_GAIN * angular))
            lens[z, 0] = c
            lens[z, 1] = s
            re, im = extend(z, spare[0], spare[1])
            spare[0] = re
            spare[1] = im
            fields[z, 0] = re
            fields[z, 1] = im

            @pl.when(z == 2)
            def _():
                forward(1)

            return carry

        lax.fori_loop(0, NZ, down, 0)
        arrive(1)
        gather(got[1], window_slot, reflect)
        spare[...] = jnp.zeros_like(spare)

        def up(step, carry):
            z = NZ - 1 - step
            weight = whole(reflect, z) * angular
            re, im = extend(z, spare[0] - weight * fields[z, 1], spare[1] + weight * fields[z, 0])
            spare[0] = re
            spare[1] = im
            return carry

        lax.fori_loop(0, NZ, up, 0)
        for part in range(SECTIONS):

            @pl.when(part * shots + shot != me)
            def _():
                remote(observed.at[0, 0], rows.at[part], row_send.at[0], row_recv.at[part], sibling).wait_recv()

            for half in range(2):
                at = (half, pl.ds(part * ROWS, ROWS))
                spare[at] = spare[at] - rows[part, half]

        def back(z, carry):
            re, im = both_sides(left_ops, right_ops, 1, spare[0], spare[1])
            c, s = lens[z, 0], lens[z, 1]
            re, im = c * re + s * im, c * im - s * re
            spare[0] = re
            spare[1] = im
            image_part = angular * (im * fields[z, 0] - re * fields[z, 1])
            partial[0] = image_part[:, :128]
            partial[1] = image_part[:, 128:]

            def cut(block_row, carry):
                for half in range(SIDE // 4):
                    parts = [partial[half, pl.ds(block_row * TL + k, 8, stride=4)] for k in range(4)]
                    for j, tile in enumerate(swap_groups(parts)):
                        tiles[block_row * SIDE + half * 4 + j] = tile
                return carry

            lax.fori_loop(0, SIDE, cut, 0)

            def put(spot, carry):
                for parity in range(2):
                    for slot in range(cap):
                        half_sums[z, parity, spot, slot] = tiles[places[(2 * spot + parity) * cap + slot]]
                return carry

            lax.fori_loop(0, count // 2, put, 0)
            swap_copy(z).start()

            @pl.when(z > 0)
            def _():
                finish_level(z - 1)

            return carry

        lax.fori_loop(0, NZ, back, 0)
        finish_level(NZ - 1)

    def sum_arrives(index, carry):
        z, source = lax.div(index, shots), lax.rem(index, shots)

        @pl.when(marcher(source, core) != me)
        def _():
            remote(
                sums.at[0, 0], got_sums.at[z, source], sum_send.at[0, 0], sum_recv.at[z, source], marcher(source, core)
            ).wait_recv()

        return carry

    lax.fori_loop(0, NZ * shots, sum_arrives, 0)

    def collect(tile, carry):
        for z in range(NZ):

            def add(source, total):
                mine = homes[tile] == blocks[source]
                return total + jnp.where(mine, got_sums[z, source, ranks[tile]], 0.0)

            total = lax.fori_loop(0, shots, add, jnp.zeros((8, 128), F32), unroll=shots <= 4)
            for chunk in range(8):
                out[tile, pl.ds(z, 1), pl.ds(chunk * 128, 128)] = total[chunk : chunk + 1]
        return carry

    lax.fori_loop(0, owned, collect, 0)

    def model_left(to, carry):
        @pl.when(marcher(to, core) != me)
        def _():
            model_copy(0, to).wait_send()
            model_copy(1, to).wait_send()

        return carry

    lax.fori_loop(0, shots, model_left, 0)
    for freq in range(NF):

        @pl.when(marcher(column, freq) != me)
        def _():
            rows_copy(freq).wait_send()

    @pl.when(computes)
    def _():
        def forwards_left(step, carry):
            forward_copy(0, step).wait_send()
            forward_copy(1, step).wait_send()
            return carry

        lax.fori_loop(0, count // 2, forwards_left, 0)

        def level_left(z, carry):
            swap_copy(z).wait_send()

            def one(step, carry):
                sum_copy(z, step).wait_send()
                return carry

            return lax.fori_loop(1, count // 2, one, carry)

        lax.fori_loop(0, NZ, level_left, 0)


def shards(wave_phase, tile_at, aperture_block, source_cell, freq_index, observed, image, slowness):
    count = lax.axis_size("tile")
    owned = image.shape[0]
    shots = count // SECTIONS
    cap = max(1, CELLS // count)
    windows = tile_at.shape[1] // SIDE
    smem = pl.BlockSpec(memory_space=pltpu.SMEM)
    vmem = pl.BlockSpec(memory_space=pltpu.VMEM)

    def ints(*shape):
        return jax.ShapeDtypeStruct(shape, jnp.int32)

    *tables, phase = pl.pallas_call(
        functools.partial(index_kernel, count, cap, owned),
        out_shape=(
            ints(shots * cap), ints(CELLS), ints(count * cap), ints(owned), ints(owned), ints(2),
            jax.ShapeDtypeStruct((1,), F32),
            jax.ShapeDtypeStruct((1, A), F32),
        ),
        in_specs=[smem, smem, smem, smem, pl.BlockSpec(memory_space=pl.ANY)],
        out_specs=(smem,) * 7 + (vmem,),
        scratch_shapes=[
            pltpu.SMEM((windows * cap,), jnp.int32),
            pltpu.SMEM((count,), jnp.int32),
            pltpu.VMEM((8, A), F32),
            pltpu.SemaphoreType.DMA,
        ],
    )(tile_at, aperture_block, source_cell, freq_index, wave_phase)

    turns = 2.0 * np.pi / A * (np.outer(np.arange(A), np.arange(A)) % A)
    table_cos = jnp.asarray(np.cos(turns), F32)
    table_sin = jnp.asarray(np.sin(turns), F32)
    dma = pltpu.SemaphoreType.DMA
    return pl.pallas_call(
        functools.partial(migrate_kernel, count, cap, owned),
        out_shape=jax.ShapeDtypeStruct((owned, NZ, TL * TL), F32),
        in_specs=[smem] * 8 + [vmem] * 6,
        out_specs=vmem,
        scratch_shapes=[
            pltpu.VMEM((2, shots * cap, 8 * NZ, 128), F32),
            pltpu.VMEM((count * cap, 8 * NZ, 128), F32),
            pltpu.VMEM((count * cap, 8 * NZ, 128), F32),
            pltpu.VMEM((SECTIONS, 2, ROWS, A), F32),
            pltpu.VMEM((NZ, 2, A, 128), F32),
            pltpu.VMEM((NZ, 2, A, 128), F32),
            pltpu.VMEM((2, A, 128), F32),
            pltpu.VMEM((NZ, 2, A, A), F32),
            pltpu.VMEM((NZ, 2, A, A), F32),
            pltpu.VMEM((2, A, A), F32),
            pltpu.VMEM((2, 2 * A, 6 * A), BF16),
            pltpu.VMEM((2, 6 * A, 2 * A), BF16),
            pltpu.VMEM((CELLS, 8, 128), F32),
            pltpu.VMEM((NZ, 2, count // 2, cap, 8, 128), F32),
            pltpu.VMEM((NZ, count // 2, cap, 8, 128), F32),
            pltpu.VMEM((NZ, count // 2, cap, 8, 128), F32),
            pltpu.VMEM((NZ, shots, cap, 8, 128), F32),
            dma((2, shots)),
            dma((2, count)),
            dma((2, count // 2)),
            dma((NF,)),
            dma((SECTIONS,)),
            dma((NZ,)),
            dma((NZ,)),
            dma((NZ, count // 2)),
            dma((NZ, shots)),
        ],
        compiler_params=pltpu.CompilerParams(collective_id=0, has_side_effects=True, vmem_limit_bytes=VMEM_LIMIT),
    )(*tables, aperture_block, phase, table_cos, table_sin, image, slowness, observed)


def solution(mesh):
    return jax.shard_map(
        shards,
        mesh=mesh,
        in_specs=(
            P(),
            P(),
            P("group"),
            P("group", None),
            P("group", None),
            P(("group", "tile"), None, None, None, None),
            P(("group", "tile"), None, None),
            P(("group", "tile"), None, None),
        ),
        out_specs=P(("group", "tile"), None, None),
        check_vma=False,
    )
```

time: 112 us -> 66 us (0.59)
  the two profiles are of different devices: /device:TPU:15 before, /device:TPU:0 now
where the time goes in v1:
time: 66 us; the launch traced here: 65.7 us
  Pallas kernels  62.2 us (94%)
  local copies, waits for them, and re-layouts  3.57 us (5%)
    pallas_call x1, Pallas kernels, shards(): pl.pallas_call(functools.partial(migrate_kernel, count, cap, owned), out_...  56.8 us
    pallas_call x1, Pallas kernels, shards(): pl.pallas_call(functools.partial(index_kernel, count, cap, owned), out_sh...  5.34 us
    unnamed x5, local copies, waits for them, and re-layouts  3.57 us

profile of v1, /device:TPU:0, one launch (start us, length us, event | category | flops | bytes accessed | tf_op | source)
XLA Modules:
  0.0 65.7 jit_solution(8025019304651652225)
XLA Ops:
  0.0 0.0 copy-start
  0.0 1.3 %copy.11.source_cell = s32[4,2]{1,0:T(4,128)} copy(s32[4,2]{0,1:T(2,128)} %param.13) | data formatting | bytes 64 | tf_op args[3]
  1.4 0.0 copy-done
  1.4 0.6 copy.12.freq_index
  2.0 5.3 %shard_map.100 = (s32[16]{0:T(128)}, s32[64]{0:T(128)}, s32[64]{0:T(128)}, s32[8]{0:T(128)}, s32[8]{0:T(128)}, /*index=5*/s32[2]{0:T(128)}, f32[1]{0:T(128)}, f32[1,256]{1,0:T(1,128)}) custom-call(s32[8,16]{1,0:T(8,128)} %tile_at.1, s32[4]{0:T(128)} %blocks.3, s32[4,2]{1,0:T(4,128)} %copy.11.source_cell, s32[4,2]{1,0:T(4,128)} %copy.12.freq_index, ...), custom_call_target="tpu_custom_call" | custom-call | tf_op jit(solution)/shard_map/pallas_call | solution.py:516
  7.3 56.8 %shard_map.101 = f32[8,4,1024]{2,1,0:T(4,128)} custom-call(s32[16]{0:T(128)} %get-tuple-element.13.picks, s32[64]{0:T(128)} %get-tuple-element.14.window_slot, s32[64]{0:T(128)} %get-tuple-element.15.places, s32[8]{0:T(128)} %get-tuple-element.16.homes, s32[8]{0:T(128)} %get-tuple-element.17.ranks, s32[2]{0:T(128)} %get-tuple-element.18.numbers, ...), custom_call_target="tpu_custom_call" | custom-call | tf_op jit(solution)/shard_map/pallas_call | solution.py:537
  64.2 1.6 %copy.14 = f32[8,4,1024]{2,1,0:T(4,128)} copy(f32[8,4,1024]{2,1,0:T(4,128)} %shard_map.101) | data formatting | bytes 262144
Async XLA Ops:
  0.0 1.4 %copy-start = (s32[4,2]{0,1:T(2,128)S(1)}, s32[4,2]{0,1:T(2,128)}, u32[]{:S(2)}) copy-start(s32[4,2]{0,1:T(2,128)} %param.14) | copy-start | bytes 100
